TPU v7x, 128 devices: a whole 4x4x4 slice. The times are simulated.
128 devices in a mesh: grp: 4 (over x_hi, core), rel: 32 (over x_lo, y, z).
Axes of the slice: x: 4 (x_hi: 2, x_lo: 2; x = x_hi * 2 + x_lo), y: 4, z: 4, core: 2. Of those that a mesh axis runs over, the one named last changes fastest.
Arguments:
- head_ids: int32 [262144], P(('grp', 'rel')), may hold values from 0 to 1023
- relations: int32 [262144, 1], P(('grp', 'rel')), may hold values from 0 to 127; in each aligned block of 2048 rows (0 to 2047, 2048 to 4095, ...) at most 32 rows name the same one
- tail_ids: int32 [262144], P(('grp', 'rel')), may hold values from 0 to 1023
- neg_owner: int32 [1], replicated, may hold values from 0 to 127
- entities: bfloat16 [131072, 512], P(('grp', 'rel')), may hold values from -0.3984375 to 0.3984375
- rel_weight: float32 [128, 512, 512], P('rel'), may hold values from -6 to 6
- rel_accum: float32 [128, 512], P('rel'), may hold values from 0.001 to 0.1
Outputs:
- losses: bfloat16 [262144], P(('grp', 'rel'))
- head_grad: bfloat16 [262144, 512], P(('grp', 'rel'))
- new_rel: float32 [128, 512, 512], P('rel')
- new_accum: float32 [128, 512], P('rel')
Inputs may be any that keep to these rules, and one draw needn't show every extreme that they name: `head_ids`: a row of the device's own shard of 1024 entity rows. `tail_ids`: a row of the device's own shard of 1024 entity rows. `relations`: in the 2048 rows of one device no relation is named by more than 32 rows; some relation is named by exactly 32. `neg_owner`: a device index, counted grp first, then rel.
All inputs are finite; a program needn't handle non-finite values.
Results may differ from a plain program's by a relative error of at most 0.0095.
Values may be sent and summed in bfloat16 or wider, within the bound.
A program may use at most 128 MiB of HBM per device.

v0:
```python
import jax
import jax.numpy as jnp
from jax import lax
from jax.sharding import PartitionSpec as P

LEARNING_RATE = 1.0


def broadcast(shard, axis, root):
    mine = lax.axis_index(axis) == root
    return lax.psum(jnp.where(mine, shard, jnp.zeros_like(shard)), axis)


def slot_ranks(rel_ids, bucket_count):
    one_hot = (rel_ids[..., None] == jnp.arange(bucket_count, dtype=jnp.int32)).astype(jnp.int32)
    running = jnp.cumsum(one_hot, axis=-2) - 1
    return jnp.sum(one_hot * running, axis=-1)


def score_rows(query_rows, tail_rows, negatives):
    positive = jnp.sum(query_rows.astype(jnp.float32) * tail_rows.astype(jnp.float32), axis=-1)
    neg_scores = jnp.dot(query_rows, negatives.T, preferred_element_type=jnp.float32)
    losses = jax.nn.softplus(-positive) + jnp.mean(jax.nn.softplus(neg_scores), axis=-1)
    coefs = (jax.nn.sigmoid(neg_scores) / negatives.shape[0]).astype(jnp.bfloat16)
    grad_query = -jax.nn.sigmoid(-positive)[:, None] * tail_rows.astype(jnp.float32)
    grad_query = grad_query + jnp.dot(coefs, negatives, preferred_element_type=jnp.float32)
    return (losses.astype(jnp.bfloat16), grad_query.astype(jnp.bfloat16))


def adagrad(weight, accumulator, gradient):
    new_accum = accumulator + jnp.mean(gradient * gradient, axis=-1)
    return (weight - LEARNING_RATE * gradient / jnp.sqrt(new_accum)[..., None], new_accum)


def to_buckets(values, position, layout):
    flat_shape = (layout[0] * layout[1] * layout[2],) + values.shape[1:]
    filled = jnp.zeros(flat_shape, values.dtype).at[position].set(values)
    return filled.reshape(layout + values.shape[1:])


def from_buckets(stacked, position):
    return stacked.reshape((-1,) + stacked.shape[3:])[position]


def per_device(head_ids, relations, tail_ids, neg_owner, entities, rel_weight, rel_accum):
    rows_here = head_ids.shape[0]
    width = entities.shape[1]
    owner_count = lax.axis_size("rel")
    local_rels = rel_weight.shape[0]
    capacity = 2 * rows_here // (owner_count * local_rels)
    layout = (owner_count, local_rels, capacity)
    rel_ids = relations[:, 0]
    position = rel_ids * capacity + slot_ranks(rel_ids, owner_count * local_rels)
    head_rows = jnp.take(entities, head_ids, axis=0)
    tail_rows = jnp.take(entities, tail_ids, axis=0)
    matrices = rel_weight.astype(jnp.bfloat16)
    negatives = broadcast(entities, ("grp", "rel"), neg_owner[0])
    held_rows, held_tails = (
        lax.all_to_all(
            to_buckets(head_rows, position, layout), "rel", split_axis=0, concat_axis=0, tiled=True
        ),
        lax.all_to_all(
            to_buckets(tail_rows, position, layout), "rel", split_axis=0, concat_axis=0, tiled=True
        ),
    )
    projected = jnp.einsum(
        "srcd,rde->srce", held_rows, matrices, preferred_element_type=jnp.float32
    ).astype(jnp.bfloat16)
    slot_losses, slot_grads = score_rows(
        projected.reshape(-1, width), held_tails.reshape(-1, width), negatives
    )
    grad_rows = slot_grads.reshape(held_rows.shape)
    partial_value = jnp.einsum(
        "srcd,srce->rde", held_rows, grad_rows, preferred_element_type=jnp.float32
    )
    head_back = jnp.einsum(
        "srce,rde->srcd", grad_rows, matrices, preferred_element_type=jnp.float32
    ).astype(jnp.bfloat16)
    partial_value, head_back = (partial_value, head_back)
    back_grads, back_losses = (
        lax.all_to_all(head_back, "rel", split_axis=0, concat_axis=0, tiled=True),
        lax.all_to_all(slot_losses.reshape(layout), "rel", split_axis=0, concat_axis=0, tiled=True),
    )
    head_grad = from_buckets(back_grads, position)
    losses = from_buckets(back_losses, position)
    grad_share = lax.psum_scatter(
        partial_value.astype(jnp.bfloat16), "grp", scatter_dimension=1, tiled=True
    ).astype(jnp.float32)
    share_rows = grad_share.shape[1]
    offset = lax.axis_index("grp") * share_rows
    weight_part = lax.dynamic_slice_in_dim(rel_weight, offset, share_rows, 1)
    accum_part = lax.dynamic_slice_in_dim(rel_accum, offset, share_rows, 1)
    weight_next, accum_next = adagrad(weight_part, accum_part, grad_share)
    new_rel, new_accum = (
        lax.all_gather(weight_next.astype(jnp.bfloat16), "grp", axis=1, tiled=True).astype(
            weight_next.dtype
        ),
        lax.all_gather(accum_next.astype(jnp.bfloat16), "grp", axis=1, tiled=True).astype(
            accum_next.dtype
        ),
    )
    return (losses, head_grad, new_rel, new_accum)


def solution(mesh):
    placed = (
        P(("grp", "rel")),
        P(("grp", "rel"), None),
        P(("grp", "rel")),
        P(),
        P(("grp", "rel"), None),
        P("rel", None, None),
        P("rel", None),
    )
    return jax.shard_map(
        per_device,
        mesh=mesh,
        in_specs=placed,
        out_specs=(
            P(("grp", "rel")),
            P(("grp", "rel"), None),
            P("rel", None, None),
            P("rel", None),
        ),
        check_vma=False,
    )
```

profile of v0, /device:TPU:73, one launch (start us, length us, event | category | flops | bytes accessed | tf_op | source)
XLA Modules:
  0.0 456.3 jit_solution(5821158530165243977)
XLA Ops:
  7.2 0.0 copy-start.1
  7.2 0.0 copy-start
  7.2 0.8 compare_and_fusion
  8.0 0.7 fusion.36
  8.7 0.8 copy.46
  9.5 0.3 fusion.30
  9.9 0.1 add_add_fusion
  10.0 0.3 copy.47
  10.3 0.0 copy-done.1
  10.3 0.6 fusion.25
  11.0 0.0 copy-done
  11.0 22.7 %scatter_custom_fusion.1 = bf16[4096,512]{1,0:T(8,128)(2,1)} fusion(s32[2048]{0:T(1024)S(1)} %bitcast.53, bf16[]{:T(256)} %constant.22.clone.1, pred[2048]{0:T(1024)(128)(4,1)S(1)} %compare_and_fusion, bf16[]{:T(256)} %constant.15.clone.2, bf16[1024,512]{1,0:T(8,128)(2,1)S(1)} %copy-done, s32[2048]{0:T(1024)S(1)} %fusion.36), kind=kCustom, calls=%fused_computation.24 | custom fusion | flops 1048576 | bytes 5253124 | tf_op jit(solution)/shard_map/scatter | solution.py:37
  33.7 0.0 copy-start.2
  33.7 8.8 %all-to-all-start.1 = ((bf16[32,4,32,512]{3,2,1,0:T(8,128)(2,1)}), bf16[32,4,32,512]{3,2,1,0:T(8,128)(2,1)}, u32[]{:S(2)}, u32[]{:S(2)}) async-start(bf16[32,4,32,512]{3,2,1,0:T(8,128)(2,1)} %bitcast.48), calls=%async_computation.1 | async-start | bytes 8388608 | tf_op jit(solution)/shard_map/all_to_all | solution.py:62
  42.5 0.0 copy-done.2
  42.5 22.6 %scatter_custom_fusion = bf16[4096,512]{1,0:T(8,128)(2,1)} fusion(s32[2048]{0:T(1024)S(1)} %bitcast.54, bf16[]{:T(256)} %constant.22.clone.1, pred[2048]{0:T(1024)(128)(4,1)S(1)} %compare_and_fusion.1, bf16[]{:T(256)} %constant.15.clone.2, bf16[1024,512]{1,0:T(8,128)(2,1)S(1)} %copy-done, s32[2048]{0:T(1024)S(1)} %fusion.35), kind=kCustom, calls=%fused_computation.26 | custom fusion | flops 1048576 | bytes 5253124 | tf_op jit(solution)/shard_map/scatter | solution.py:37
  65.2 26.2 %all-to-all-done.1 = bf16[32,4,32,512]{3,2,1,0:T(8,128)(2,1)} async-done(((bf16[32,4,32,512]{3,2,1,0:T(8,128)(2,1)}), bf16[32,4,32,512]{3,2,1,0:T(8,128)(2,1)}, u32[]{:S(2)}, u32[]{:S(2)}) %all-to-all-start.1) | async-done | bytes 4194336 | tf_op jit(solution)/shard_map/all_to_all | solution.py:62
  91.4 12.9 %all-to-all-start = ((bf16[32,4,32,512]{3,2,1,0:T(8,128)(2,1)}), bf16[32,4,32,512]{3,2,1,0:T(8,128)(2,1)}, u32[]{:S(2)}, u32[]{:S(2)}) async-start(bf16[32,4,32,512]{3,2,1,0:T(8,128)(2,1)} %bitcast.47), calls=%async_computation | async-start | bytes 8388608 | tf_op jit(solution)/shard_map/all_to_all | solution.py:59
  104.4 0.0 all-reduce.2.cloned.1.call-start
  105.1 1.0 broadcast_select_fusion
  106.1 0.0 all-reduce.2.cloned.1.call-update
  106.2 0.0 reduce-scatter.2.cloned.1.call-start
  106.2 48.3 %all-to-all-done = bf16[32,4,32,512]{3,2,1,0:T(8,128)(2,1)} async-done(((bf16[32,4,32,512]{3,2,1,0:T(8,128)(2,1)}), bf16[32,4,32,512]{3,2,1,0:T(8,128)(2,1)}, u32[]{:S(2)}, u32[]{:S(2)}) %all-to-all-start) | async-done | bytes 4194336 | tf_op jit(solution)/shard_map/all_to_all | solution.py:59
  154.5 7.2 %multiply_reduce_fusion = (f32[32,4,32]{2,0,1:T(8,128)S(1)}, bf16[32,4,32,512]{3,2,0,1:T(8,128)(2,1)S(1)}) fusion(bf16[32,4,32,512]{3,2,1,0:T(8,128)(2,1)} %all-to-all-done.1, f32[4,512,512]{2,1,0:T(8,128)} %param.14, bf16[32,4,32,512]{3,2,1,0:T(8,128)(2,1)} %all-to-all-done), kind=kOutput, calls=%fused_computation.12 | convolution fusion | flops 2159013888 | bytes 16793600 | tf_op jit(solution)/shard_map/srcd,rde->srce/dot_general | solution.py:66
  161.6 2.5 copy.50
  164.1 3.4 copy_convert_fusion
  167.6 4.3 copy.54
  171.9 115.8 %all-reduce.2.cloned.1.call-done = bf16[1024,512]{1,0:T(8,128)(2,1)} async-done(((bf16[1024,512]{1,0:T(8,128)(2,1)}), bf16[1024,512]{1,0:T(8,128)(2,1)}) %all-reduce.2.cloned.1.call-update) | async-done | bytes 1048592 | tf_op jit(solution)/shard_map/psum | solution.py:11
  287.7 0.0 copy-start.3
  287.7 16.7 %fusion = (f32[4096]{0:T(1024)S(1)}, f32[4096,1024]{0,1:T(8,128)}) fusion(bf16[4096,512]{1,0:T(8,128)(2,1)} %bitcast.49, bf16[1024,512]{1,0:T(8,128)(2,1)} %all-reduce.2.cloned.1.call-done), kind=kOutput, calls=%fused_computation.7 | convolution fusion | flops 4324323328 | bytes 22036480 | tf_op jit(solution)/shard_map/dot_general | solution.py:22
  304.4 0.1 div.41
  304.5 0.1 divide_negate_fusion
  304.6 0.1 neg.33
  304.7 0.0 copy-done.3
  304.7 11.2 %fusion.2 = bf16[4096,512]{1,0:T(8,128)(2,1)S(1)} fusion(f32[32,4,32,512]{3,2,1,0:T(8,128)} %copy.54, bf16[1024,512]{1,0:T(8,128)(2,1)S(1)} %copy-done.3, f32[4096,1024]{0,1:T(8,128)} %get-tuple-element.12, f32[4096]{0:T(1024)S(1)} %neg.33), kind=kOutput, calls=%fused_computation.11 | convolution fusion | flops 4322230272 | bytes 30425088 | tf_op jit(solution)/shard_map/dot_general | solution.py:26
  315.9 0.0 copy-start.4
  315.9 2.0 copy-done.4
  317.9 5.9 %bitcast_convert_fusion = bf16[4,512,512]{2,1,0:T(8,128)(2,1)} fusion(bf16[32,4,32,512]{3,2,1,0:T(8,128)(2,1)} %all-to-all-done, bf16[32,4,32,512]{3,2,1,0:T(8,128)(2,1)S(1)} %bitcast.56), kind=kOutput, calls=%fused_computation.14 | convolution fusion | flops 2148532224 | bytes 10485760 | tf_op jit(solution)/shard_map/srcd,srce->rde/dot_general | solution.py:73
  323.8 0.0 reduce-scatter.2.cloned.1.call-update
  323.8 0.6 copy.52
  324.4 7.5 %all-to-all-start.2 = ((bf16[32,4,32]{2,1,0:T(4,128)(2,1)}), bf16[32,4,32]{2,1,0:T(4,128)(2,1)S(1)}, u32[]{:S(2)}, u32[]{:S(2)}) async-start(bf16[32,4,32]{2,1,0:T(4,128)(2,1)} %copy.52), calls=%async_computation.2 | async-start | bytes 65536 | tf_op jit(solution)/shard_map/all_to_all | solution.py:82
  331.9 6.5 %convert_bitcast_fusion = bf16[32,4,32,512]{3,2,0,1:T(8,128)(2,1)S(1)} fusion(bf16[32,4,32,512]{3,2,1,0:T(8,128)(2,1)} %bitcast.57, f32[4,512,512]{2,1,0:T(8,128)} %param.14), kind=kOutput, calls=%fused_computation.20 | convolution fusion | flops 2150629376 | bytes 12582912 | tf_op jit(solution)/shard_map/srce,rde->srcd/dot_general | solution.py:76
  338.4 2.3 copy.56
  340.8 0.0 all-to-all-done.2
  340.8 7.8 %all-to-all-start.3 = ((bf16[32,4,32,512]{3,2,1,0:T(8,128)(2,1)}), bf16[32,4,32,512]{3,2,1,0:T(8,128)(2,1)}, u32[]{:S(2)}, u32[]{:S(2)}) async-start(bf16[32,4,32,512]{3,2,1,0:T(8,128)(2,1)} %copy.56), calls=%async_computation.3 | async-start | bytes 8388608 | tf_op jit(solution)/shard_map/all_to_all | solution.py:81
  348.6 0.0 all-gather.2.cloned.1.call-start
  348.6 22.8 %reduce-scatter.2.cloned.1.call-done = bf16[4,128,512]{2,1,0:T(8,128)(2,1)} async-done(((bf16[4,512,512]{2,1,0:T(8,128)(2,1)}), bf16[4,128,512]{2,1,0:T(8,128)(2,1)}) %reduce-scatter.2.cloned.1.call-update) | async-done | bytes 524304 | tf_op jit(solution)/shard_map/reduce_scatter | solution.py:86
  371.4 1.2 fusion.22
  372.7 0.7 fusion.37
  373.4 2.4 fusion.24
  375.8 0.0 all-gather.2.cloned.1.call-update
  375.8 0.1 reshape.81
  375.9 22.1 %gather_fusion = bf16[2048]{0:T(1024)(128)(2,1)} fusion(bf16[4096]{0:T(1024)(128)(2,1)S(1)} %reshape.81, s32[2048]{0:T(1024)S(1)} %broadcast_clamp_fusion), kind=kCustom, calls=%fused_computation.2 | custom fusion | bytes 16384 | tf_op jit(solution)/shard_map/gather | solution.py:42
  398.0 27.7 %all-to-all-done.3 = bf16[32,4,32,512]{3,2,1,0:T(8,128)(2,1)} async-done(((bf16[32,4,32,512]{3,2,1,0:T(8,128)(2,1)}), bf16[32,4,32,512]{3,2,1,0:T(8,128)(2,1)}, u32[]{:S(2)}, u32[]{:S(2)}) %all-to-all-start.3) | async-done | bytes 4194336 | tf_op jit(solution)/shard_map/all_to_all | solution.py:81
  425.7 12.0 %gather_fusion.1 = bf16[2048,512]{1,0:T(8,128)(2,1)} fusion(bf16[4096,512]{1,0:T(8,128)(2,1)} %bitcast.18, s32[2048]{0:T(1024)S(1)} %broadcast_clamp_fusion), kind=kCustom, calls=%fused_computation.3 | custom fusion | bytes 4202496 | tf_op jit(solution)/shard_map/gather | solution.py:42
  437.7 7.1 %all_gather.7 = bf16[4,512]{1,0:T(4,128)(2,1)S(1)} all-gather(bf16[4,128]{1,0:T(4,128)(2,1)S(1)} %get-tuple-element.7), channel_id=1, replica_groups=mesh['grp'=4,'rel'=32] {'grp'}, dimensions={1}, use_global_device_ids=true | all-gather | bytes 5120 | tf_op jit(solution)/shard_map/all_gather | solution.py:98
  444.8 0.6 convert_element_type.80
  445.4 0.0 all-gather.2.cloned.1.call-done
  445.4 4.2 convert_element_type.78
  (9 shorter events, 0.1 us)
Async XLA Ops:
  7.2 3.1 copy-start.1
  7.2 3.8 copy-start
  33.7 8.9 %copy-start.2 = (s32[2048]{0:T(1024)S(1)}, s32[2048]{0:T(1024)}, u32[]{:S(2)}) copy-start(s32[2048]{0:T(1024)} %param.9) | copy-start | bytes 24580
  33.7 57.8 %all-to-all-start.1 = ((bf16[32,4,32,512]{3,2,1,0:T(8,128)(2,1)}), bf16[32,4,32,512]{3,2,1,0:T(8,128)(2,1)}, u32[]{:S(2)}, u32[]{:S(2)}) async-start(bf16[32,4,32,512]{3,2,1,0:T(8,128)(2,1)} %bitcast.48), calls=%async_computation.1 | async-start | bytes 8388608 | tf_op jit(solution)/shard_map/all_to_all | solution.py:62
  91.4 63.0 %all-to-all-start = ((bf16[32,4,32,512]{3,2,1,0:T(8,128)(2,1)}), bf16[32,4,32,512]{3,2,1,0:T(8,128)(2,1)}, u32[]{:S(2)}, u32[]{:S(2)}) async-start(bf16[32,4,32,512]{3,2,1,0:T(8,128)(2,1)} %bitcast.47), calls=%async_computation | async-start | bytes 8388608 | tf_op jit(solution)/shard_map/all_to_all | solution.py:59
  104.4 183.3 %all-reduce.2.cloned.1.call-start = ((), (), s32[]{:S(2)}) async-start(), calls=%async_computation.5 | async-start | bytes 2097152 | tf_op jit(solution)/shard_map/psum | solution.py:11
  106.2 265.3 %reduce-scatter.2.cloned.1.call-start = ((), (), s32[]{:S(2)}) async-start(), calls=%async_computation.6 | async-start | bytes 2621440 | tf_op jit(solution)/shard_map/reduce_scatter | solution.py:86
  287.7 17.0 %copy-start.3 = (bf16[1024,512]{1,0:T(8,128)(2,1)S(1)}, bf16[1024,512]{1,0:T(8,128)(2,1)}, u32[]{:S(2)}) copy-start(bf16[1024,512]{1,0:T(8,128)(2,1)} %all-reduce.2.cloned.1.call-done) | copy-start | bytes 3145732
  315.9 2.0 copy-start.4
  324.4 16.3 %all-to-all-start.2 = ((bf16[32,4,32]{2,1,0:T(4,128)(2,1)}), bf16[32,4,32]{2,1,0:T(4,128)(2,1)S(1)}, u32[]{:S(2)}, u32[]{:S(2)}) async-start(bf16[32,4,32]{2,1,0:T(4,128)(2,1)} %copy.52), calls=%async_computation.2 | async-start | bytes 65536 | tf_op jit(solution)/shard_map/all_to_all | solution.py:82
  340.8 85.0 %all-to-all-start.3 = ((bf16[32,4,32,512]{3,2,1,0:T(8,128)(2,1)}), bf16[32,4,32,512]{3,2,1,0:T(8,128)(2,1)}, u32[]{:S(2)}, u32[]{:S(2)}) async-start(bf16[32,4,32,512]{3,2,1,0:T(8,128)(2,1)} %copy.56), calls=%async_computation.3 | async-start | bytes 8388608 | tf_op jit(solution)/shard_map/all_to_all | solution.py:81
  348.6 96.8 %all-gather.2.cloned.1.call-start = ((), (), s32[]{:S(2)}) async-start(), calls=%async_computation.7 | async-start | bytes 2621440 | tf_op jit(solution)/shard_map/all_gather | solution.py:95
Sparse Core Ops, SparseCore 0:
  110.6 177.0 all-reduce.1
  323.9 47.4 reduce-scatter.1
  375.9 40.6 all-gather.1
where the time goes:
time: 464 us; the launch traced here: 456 us
  waiting for transfers between devices  241 us (52%)
  other arithmetic  61.6 us (13%)
  matrix products  47.4 us (10%)
  local copies, waits for them, and re-layouts  47.3 us (10%)
  starting transfers between devices  37.2 us (8%)
  between operations  14.8 us (3%)
  blocking collectives  7.07 us (2%)
    psum x1, waiting for transfers between devices, broadcast(): return lax.psum(jnp.where(mine, shard, jnp.zeros_like(shard)), axis)  116 us
    all_to_all x1, waiting for transfers between devices, per_device(): lax.all_to_all(to_buckets(head_rows, position, layout), 'rel', split_axis...  48.3 us
    scatter x2, other arithmetic, to_buckets(): filled = jnp.zeros(flat_shape, values.dtype).at[position].set(values)  45.3 us
    gather x2, local copies, waits for them, and re-layouts, from_buckets(): return stacked.reshape((-1,) + stacked.shape[3:])[position]  34.1 us
    all_to_all x1, waiting for transfers between devices, per_device(): lax.all_to_all(head_back, 'rel', split_axis=0, concat_axis=0, tiled=True)  27.7 us
    all_to_all x1, waiting for transfers between devices, per_device(): lax.all_to_all(to_buckets(tail_rows, position, layout), 'rel', split_axis...  26.2 us
    reduce_scatter x1, waiting for transfers between devices, per_device(): lax.psum_scatter(partial_value.astype(jnp.bfloat16), 'grp', scatter_dimen...  22.8 us
    dot_general x1, matrix products, score_rows(): jnp.dot(query_rows, negatives.T, preferred_element_type=jnp.float32)  16.7 us
  transfers between devices with their start and end apart: 7, of which 5 were waited for; matrix products, arithmetic and copies ran while one was open for 20% of the time, Pallas kernels for 0%

commit v1 on v0

v1 whole, which is shorter than its diff:
```python
import jax
import jax.numpy as jnp
from jax import lax
from jax.experimental import pallas as pl
from jax.experimental.pallas import tpu as pltpu
from jax.sharding import PartitionSpec as P

MESH = pl.DeviceIdType.MESH
BF, F32, I32 = jnp.bfloat16, jnp.float32, jnp.int32
ROWS, WIDTH, NEG = 2048, 512, 1024
CHUNKS, PEERS, CAP = 4, 32, 32
VMEM_BYTES = 58 * 2**20


def place():
    grp, rel = lax.axis_index("grp"), lax.axis_index("rel")
    x_hi, core = grp // 2, grp % 2
    x_lo, y, z = rel // 16, (rel // 4) % 4, rel % 4
    return x_hi, core, x_hi * 2 + x_lo, x_lo, y, z


def device_at(core, x, y, z):
    return ((x // 2) * 2 + core, (x % 2) * 16 + y * 4 + z)


def split_shift(n):
    b = (n * 5) % PEERS
    return b // 16, (b // 4) % 4, b % 4


def peer(n, sign, here):
    x_hi, core, x, x_lo, y, z = here
    dx, dy, dz = split_shift(n)
    x = (x + dx * (1 + 2 * (x % 2) + 2 * ((dy + dz) % 2))) % 4
    return device_at(core, x, (y + sign * dy + 4) % 4, (z + sign * dz + 4) % 4)


def prep_kernel(rel_ref, head_ref, tail_ref, table_ref, pos_ref):
    x_hi, core, x, x_lo, y, z = place()
    size = 256
    lane = lax.broadcasted_iota(I32, (size, 128), 1)
    lower = lax.broadcasted_iota(I32, (size, size), 0) > lax.broadcasted_iota(I32, (size, size), 1)
    lower = jnp.where(lower, 1.0, 0.0).astype(BF)

    def block(i, carry):
        seen, table = carry
        rows = pl.ds(pl.multiple_of(i * size, size), size)
        rel, head, tail = rel_ref[rows, :], head_ref[rows, :] + 1, tail_ref[rows, :] + 1
        hot = jnp.where(rel == lane, 1.0, 0.0)
        before = jnp.dot(lower, hot.astype(BF), preferred_element_type=F32) + seen
        rank = jnp.sum(hot * before, axis=1, keepdims=True).astype(I32)
        digit = jnp.where(lane < 64, jnp.where(lane < 32, head // 32, head % 32), jnp.where(lane < 96, tail // 32, tail % 32))
        marks = jnp.where(lane % 32 == rank, digit, 0).astype(F32).astype(BF)
        table = table + lax.dot_general(marks, hot.astype(BF), (((0,), (0,)), ((), ())), preferred_element_type=F32)
        owner = rel // 4
        b = ((owner // 16 + 2 - x_lo) % 2) * 16 + ((owner // 4 % 4 + 4 - y) % 4) * 4 + (owner % 4 + 4 - z) % 4
        pos_ref[rows, :] = (rel % 4) * (PEERS * CAP) + (b * 13 % PEERS) * CAP + rank
        return seen + jnp.sum(hot, axis=0, keepdims=True), table

    start = (jnp.zeros((1, 128), F32), jnp.zeros((128, 128), F32))
    _, table = lax.fori_loop(0, ROWS // size, block, start)
    table_ref[0:32, :] = table[0:32] * 32.0 + table[32:64] - 1.0
    table_ref[32:64, :] = table[64:96] * 32.0 + table[96:128] - 1.0


def main_kernel(
    owner_ref, ent_ref, table_ref, pos_ref, accum_ref, weight_ref,
    grad_ref, loss_ref, rel_ref, acc_ref,
    out_rows, in_rows, out_back, in_back, out_loss, in_loss, w32, w16, gbuf, lrow,
    own, g1s, g1r, g2s, g2r,
    neg, n0s, n0r, n1, n1r, n2, n2r, n3, n3r, n4,
    w_sem, rows_ss, rows_rs, back_ss, back_rs, loss_ss, loss_rs,
    neg_ss, neg_rs, grp_ss, grp_rs,
):
    here = place()
    x_hi, core, x, x_lo, y, z = here
    me = lax.axis_index("grp") * PEERS + lax.axis_index("rel")
    mate = device_at(1 - core, x, y, z)
    across = device_at(core, (x + 2) % 4, y, z)
    beside = device_at(core, (x + 3 + 2 * (x % 2)) % 4, y, z)
    quarter = core * 2 + x_hi

    def remote(src, dst, ss, rs, device):
        return pltpu.make_async_remote_copy(src_ref=src, dst_ref=dst, send_sem=ss, recv_sem=rs, device_id=device, device_id_type=MESH)

    w_copy = pltpu.make_async_copy(weight_ref, w32, w_sem)
    w_copy.start()

    barrier = pltpu.get_barrier_semaphore()

    def greet(n, c):
        pl.semaphore_signal(barrier, inc=1, device_id=peer(n, 1, here), device_id_type=MESH)
        return c

    lax.fori_loop(1, PEERS, greet, 0)
    for device in (mate, across, beside):
        pl.semaphore_signal(barrier, inc=1, device_id=device, device_id_type=MESH)
    pl.semaphore_wait(barrier, PEERS + 2)

    mine = (owner_ref[0] == me).astype(F32).astype(BF)

    def ring(axis, d):
        if axis == 0:
            return device_at(core, (x + d) % 4, y, z), (x + d) % 4
        if axis == 1:
            return device_at(core, x, (y + d) % 4, z), (y + d) % 4
        return device_at(core, x, y, (z + d) % 4), (z + d) % 4

    def rows_of(start, size):
        return pl.ds(pl.multiple_of(start, size), size)

    block32 = core * 512 + x * 128 + y * 32

    def neg_copies(stage):
        if stage == 0:
            return [remote(n0s, n0r, neg_ss.at[0, 0], neg_rs.at[0, 0], mate)]
        if stage == 6:
            part = neg.at[rows_of(core * 512, 512)]
            return [remote(part, part, neg_ss.at[6, 0], neg_rs.at[6, 0], mate)]
        copies = []
        for d in (1, 2, 3):
            sems = neg_ss.at[stage, d - 1], neg_rs.at[stage, d - 1]
            device, there = ring({1: 0, 2: 1, 3: 2, 4: 1, 5: 0}[stage], d)
            if stage == 1:
                copies.append(remote(n1.at[rows_of(there * 128, 128)], n1r.at[d - 1], *sems, device))
            elif stage == 2:
                copies.append(remote(n2.at[rows_of(there * 32, 32)], n2r.at[d - 1], *sems, device))
            elif stage == 3:
                copies.append(remote(n3, n3r.at[d - 1], *sems, device))
            elif stage == 4:
                copies.append(remote(n4, neg.at[rows_of(block32, 32)], *sems, device))
            else:
                part = neg.at[rows_of(core * 512 + x * 128, 128)]
                copies.append(remote(part, part, *sems, device))
        return copies

    def neg_start(stage):
        if stage == 0:
            n0s[...] = ent_ref[rows_of((1 - core) * 512, 512), :] * mine
        elif stage == 1:
            n1[...] = ent_ref[rows_of(core * 512, 512), :] * mine + n0r[...]
        elif stage == 2:
            n2[...] = n1[rows_of(x * 128, 128), :] + n1r[0] + n1r[1] + n1r[2]
        elif stage == 3:
            n3[...] = n2[rows_of(y * 32, 32), :] + n2r[0] + n2r[1] + n2r[2]
        elif stage == 4:
            total = n3[...] + n3r[0] + n3r[1] + n3r[2]
            n4[...] = total
            neg[rows_of(block32, 32), :] = total
        for copy in neg_copies(stage):
            copy.start()

    def neg_wait(stage):
        for copy in neg_copies(stage):
            copy.wait()

    def rows_copy(j, n, sign):
        return remote(out_rows.at[j, n], in_rows.at[j, n], rows_ss.at[j, n], rows_rs.at[j, n], peer(n, sign, here))

    lane128 = lax.broadcasted_iota(I32, (64, 128), 1)
    lane1024 = lax.broadcasted_iota(I32, (64, NEG), 1).astype(F32)

    def send_rows(j, step):
        hots = []
        for m in range(4):
            _, owner = peer(step * 4 + m, 1, here)
            ids = jnp.sum(jnp.where(lane128 == owner * 4 + j, table_ref[...], 0.0), axis=1, keepdims=True)
            hots.append(jnp.where(lane1024 == ids, 1.0, 0.0).astype(BF))
        rows = jnp.dot(jnp.concatenate(hots, axis=0), ent_ref[...], preferred_element_type=F32).astype(BF)
        out_rows[j, pl.ds(step * 4, 4)] = rows.reshape(4, 64, WIDTH)
        for m in range(4):
            if m == 0:

                @pl.when(step == 0)
                def _():
                    in_rows[j, 0] = rows[0:64]

                @pl.when(step > 0)
                def _():
                    rows_copy(j, step * 4, 1).start()

            else:
                rows_copy(j, step * 4 + m, 1).start()

    def send_steps(first, last):
        def body(i, c):
            send_rows(i // 8, i % 8)
            return c

        lax.fori_loop(first, last, body, 0)

    neg_start(0)
    for stage in range(7):
        send_steps(2 * stage, 2 * stage + 2)
        neg_wait(stage)
        if stage < 6:
            neg_start(stage + 1)
    send_steps(14, 32)
    w_copy.wait()

    nt = (((1,), (1,)), ((), ()))
    tn = (((0,), (0,)), ((), ()))

    def back_copy(j, n, sign):
        return remote(out_back.at[j, n], in_back.at[j, n], back_ss.at[j, n], back_rs.at[j, n], peer(n, sign, here))

    def loss_copy(j, n, sign):
        tile = pl.ds(pl.multiple_of((n // 4) * 128, 128), 128)
        return remote(out_loss.at[j, :, tile], in_loss.at[j, n], loss_ss.at[j, n], loss_rs.at[j, n], peer(n, sign, here))

    def score(j, mb, c):
        for k in range(8):
            if k == 0:

                @pl.when(mb > 0)
                def _():
                    rows_copy(j, mb * 8, -1).wait_recv()

            else:
                rows_copy(j, mb * 8 + k, -1).wait_recv()
        peers = pl.ds(mb * 8, 8)
        h = in_rows[j, peers, 0:32, :].reshape(256, WIDTH)
        t = in_rows[j, peers, 32:64, :].reshape(256, WIDTH).astype(F32)
        q = jnp.dot(h, w16[...], preferred_element_type=F32).astype(BF)
        pos = jnp.sum(q.astype(F32) * t, axis=1, keepdims=True)
        s = lax.dot_general(q, neg[...], nt, preferred_element_type=F32)
        e = jnp.exp(-jnp.abs(s))
        soft = jnp.maximum(s, 0.0) + jnp.log1p(e)
        inv = 1.0 / (1.0 + e)
        coef = (jnp.where(s >= 0.0, inv, e * inv) * (1.0 / NEG)).astype(BF)
        g = jnp.dot(coef, neg[...], preferred_element_type=F32)
        ep = jnp.exp(-jnp.abs(pos))
        loss = jnp.maximum(-pos, 0.0) + jnp.log1p(ep) + jnp.sum(soft, axis=1, keepdims=True) * (1.0 / NEG)
        g = (g - jnp.where(pos <= 0.0, 1.0, ep) / (1.0 + ep) * t).astype(BF)
        gbuf[pl.ds(pl.multiple_of(mb * 256, 256), 256), :] = g
        back = lax.dot_general(g, w16[...], nt, preferred_element_type=F32).astype(BF)
        out_back[j, peers] = back.reshape(8, CAP, WIDTH)
        spot = lax.broadcasted_iota(I32, (256, 128), 1) == 0
        column = jnp.where(spot, loss, 0.0).astype(BF)
        row = lax.dot_general(jnp.ones((16, 128), BF), column, nt, preferred_element_type=F32).astype(BF)
        out_loss[j, :, pl.ds(pl.multiple_of(mb * 256, 256), 256)] = row

        @pl.when(mb == 0)
        def _():
            in_back[j, 0] = back[0:CAP]
            in_loss[j, 0] = row[:, 0:128]

        for k in range(8):
            if k == 0:

                @pl.when(mb > 0)
                def _():
                    back_copy(j, mb * 8, -1).start()
                    loss_copy(j, mb * 8, -1).start()

            else:
                back_copy(j, mb * 8 + k, -1).start()
                loss_copy(j, mb * 8 + k, -1).start()
        return c

    def g1_copy(j):
        return remote(g1s.at[j], g1r.at[j], grp_ss.at[0, j], grp_rs.at[0, j], mate)

    def g2_copy(j):
        return remote(g2s.at[j], g2r.at[j], grp_ss.at[1, j], grp_rs.at[1, j], across)

    def g3_copies(j):
        part = rel_ref.at[j, rows_of(quarter * 128, 128)]
        tile = acc_ref.at[j, quarter]
        return (
            remote(part, part, grp_ss.at[2, j], grp_rs.at[2, j], across),
            remote(tile, tile, grp_ss.at[3, j], grp_rs.at[3, j], across),
        )

    def g4_copies(j):
        part = rel_ref.at[j, rows_of(core * 256, 256)]
        tile = acc_ref.at[j, pl.ds(core * 2, 2)]
        return (
            remote(part, part, grp_ss.at[4, j], grp_rs.at[4, j], mate),
            remote(tile, tile, grp_ss.at[5, j], grp_rs.at[5, j], mate),
        )

    def partial(j):
        for half, mine_too in ((1 - core, False), (core, True)):
            columns = pl.ds(pl.multiple_of(half * 256, 256), 256)
            h = in_rows[j, :, 0:32, columns].reshape(PEERS * CAP, 256)
            value = lax.dot_general(h, gbuf[...], tn, preferred_element_type=F32)
            if mine_too:
                own[j] = value
            else:
                g1s[j] = value.astype(BF)
                g1_copy(j).start()

    def g1_finish(j):
        g1_copy(j).wait_recv()
        other = rows_of((1 - x_hi) * 128, 128)
        g2s[j] = (own[j, other, :] + g1r[j, other, :].astype(F32)).astype(BF)
        g2_copy(j).start()

    def g2_finish(j):
        g2_copy(j).wait_recv()
        keep = rows_of(x_hi * 128, 128)
        total = own[j, keep, :] + g1r[j, keep, :].astype(F32) + g2r[j].astype(F32)
        eye = lax.broadcasted_iota(I32, (128, 128), 0) == lax.broadcasted_iota(I32, (128, 128), 1)
        before = accum_ref[j : j + 1, pl.ds(pl.multiple_of(quarter * 128, 128), 128)]
        before = jnp.sum(jnp.where(eye, before, 0.0), axis=1, keepdims=True)
        after = before + jnp.sum(total * total, axis=1, keepdims=True) * (1.0 / WIDTH)
        rows = rows_of(quarter * 128, 128)
        rel_ref[j, rows, :] = (w32[j, rows, :] - total / jnp.sqrt(after)).astype(BF)
        line = jnp.sum(jnp.where(eye, after, 0.0), axis=0, keepdims=True)
        acc_ref[j, quarter] = jnp.broadcast_to(line, (8, 128))
        for copy in g3_copies(j):
            copy.start()

    def g3_finish(j):
        for copy in g3_copies(j):
            copy.wait_recv()
        for copy in g4_copies(j):
            copy.start()

    def collect(j):
        def arrive(n, c):
            back_copy(j, n, 1).wait_recv()
            loss_copy(j, n, 1).wait_recv()
            return c

        lax.fori_loop(1, PEERS, arrive, 0)
        group = lax.broadcasted_iota(I32, (16, 128), 1) // CAP
        for tile in range(8):
            value = jnp.zeros((16, 128), F32)
            for m in range(4):
                value = jnp.where(group == m, in_loss[j, tile * 4 + m].astype(F32), value)
            lrow[:, tile * 128 : tile * 128 + 128] = value.astype(BF)

        def block(i, c):
            rows = pl.ds(pl.multiple_of(i * 256, 256), 256)
            slot = lax.broadcasted_iota(I32, (256, PEERS * CAP), 1) + j * (PEERS * CAP)
            pick = jnp.where(pos_ref[rows, :] == slot, 1.0, 0.0).astype(BF)
            stack = in_back[j].reshape(PEERS * CAP, WIDTH)
            part = jnp.dot(pick, stack, preferred_element_type=F32).astype(BF)
            losses = lax.dot_general(lrow[...], pick, nt, preferred_element_type=F32)
            if j == 0:
                grad_ref[rows, :] = part
                loss_ref[:, rows] = losses
            else:
                grad_ref[rows, :] = grad_ref[rows, :] + part
                loss_ref[:, rows] = loss_ref[:, rows] + losses
            return c

        lax.fori_loop(0, ROWS // 256, block, 0)

    for j in range(CHUNKS):
        w16[...] = w32[j].astype(BF)
        lax.fori_loop(0, 4, lambda mb, c, j=j: score(j, mb, c), 0)
        partial(j)
        if j >= 1:
            g2_finish(j - 1)
        if j >= 2:
            g3_finish(j - 2)
        if j >= 1:
            collect(j - 1)
        g1_finish(j)
    g3_finish(2)
    g2_finish(3)
    collect(3)
    g3_finish(3)
    for j in range(CHUNKS):
        for copy in g4_copies(j):
            copy.wait_recv()

    def drain(i, c):
        j, n = i // PEERS, i % PEERS

        @pl.when(n > 0)
        def _():
            rows_copy(j, n, 1).wait_send()
            back_copy(j, n, -1).wait_send()
            loss_copy(j, n, -1).wait_send()

        return c

    lax.fori_loop(0, CHUNKS * PEERS, drain, 0)
    for j in range(CHUNKS):
        for copy in (g1_copy(j), g2_copy(j), *g3_copies(j), *g4_copies(j)):
            copy.wait_send()


def per_device(head_ids, relations, tail_ids, neg_owner, entities, rel_weight, rel_accum):
    vmem = pl.BlockSpec(memory_space=pltpu.VMEM)
    table, position = pl.pallas_call(
        prep_kernel,
        out_shape=(jax.ShapeDtypeStruct((64, 128), F32), jax.ShapeDtypeStruct((ROWS, 1), I32)),
        in_specs=[vmem] * 3,
        out_specs=(vmem, vmem),
        name="prep",
    )(relations, head_ids.reshape(ROWS, 1), tail_ids.reshape(ROWS, 1))
    dma = pltpu.SemaphoreType.DMA
    scratch = [
        pltpu.VMEM((CHUNKS, PEERS, 64, WIDTH), BF),
        pltpu.VMEM((CHUNKS, PEERS, 64, WIDTH), BF),
        pltpu.VMEM((CHUNKS, PEERS, CAP, WIDTH), BF),
        pltpu.VMEM((CHUNKS, PEERS, CAP, WIDTH), BF),
        pltpu.VMEM((CHUNKS, 16, PEERS * CAP), BF),
        pltpu.VMEM((CHUNKS, PEERS, 16, 128), BF),
        pltpu.VMEM((CHUNKS, WIDTH, WIDTH), F32),
        pltpu.VMEM((WIDTH, WIDTH), BF),
        pltpu.VMEM((PEERS * CAP, WIDTH), BF),
        pltpu.VMEM((16, PEERS * CAP), BF),
        pltpu.VMEM((CHUNKS, 256, WIDTH), F32),
        pltpu.VMEM((CHUNKS, 256, WIDTH), BF),
        pltpu.VMEM((CHUNKS, 256, WIDTH), BF),
        pltpu.VMEM((CHUNKS, 128, WIDTH), BF),
        pltpu.VMEM((CHUNKS, 128, WIDTH), BF),
        pltpu.VMEM((NEG, WIDTH), BF),
        pltpu.VMEM((512, WIDTH), BF),
        pltpu.VMEM((512, WIDTH), BF),
        pltpu.VMEM((512, WIDTH), BF),
        pltpu.VMEM((3, 128, WIDTH), BF),
        pltpu.VMEM((128, WIDTH), BF),
        pltpu.VMEM((3, 32, WIDTH), BF),
        pltpu.VMEM((32, WIDTH), BF),
        pltpu.VMEM((3, 32, WIDTH), BF),
        pltpu.VMEM((32, WIDTH), BF),
        dma,
        *[dma((CHUNKS, PEERS))] * 6,
        *[dma((7, 3))] * 2,
        *[dma((6, CHUNKS))] * 2,
    ]
    head_grad, losses, new_rel, new_accum = pl.pallas_call(
        main_kernel,
        out_shape=(
            jax.ShapeDtypeStruct((ROWS, WIDTH), BF),
            jax.ShapeDtypeStruct((16, ROWS), F32),
            jax.ShapeDtypeStruct((CHUNKS, WIDTH, WIDTH), BF),
            jax.ShapeDtypeStruct((CHUNKS, 4, 8, 128), F32),
        ),
        in_specs=[pl.BlockSpec(memory_space=pltpu.SMEM), vmem, vmem, vmem, vmem, pl.BlockSpec(memory_space=pl.ANY)],
        out_specs=(vmem,) * 4,
        scratch_shapes=scratch,
        compiler_params=pltpu.CompilerParams(collective_id=0, has_side_effects=True, vmem_limit_bytes=VMEM_BYTES),
        name="rescal",
    )(neg_owner, entities, table, position, rel_accum, rel_weight)
    return (
        losses[0].astype(BF),
        head_grad,
        new_rel.astype(F32),
        new_accum[:, :, 0, :].reshape(CHUNKS, WIDTH),
    )


def solution(mesh):
    placed = (
        P(("grp", "rel")),
        P(("grp", "rel"), None),
        P(("grp", "rel")),
        P(),
        P(("grp", "rel"), None),
        P("rel", None, None),
        P("rel", None),
    )
    return jax.shard_map(
        per_device,
        mesh=mesh,
        in_specs=placed,
        out_specs=(
            P(("grp", "rel")),
            P(("grp", "rel"), None),
            P("rel", None, None),
            P("rel", None),
        ),
        check_vma=False,
    )
```

time: 464 us -> 227 us (0.49)
  the two profiles are of different devices: /device:TPU:73 before, /device:TPU:33 now
where the time goes in v1:
time: 227 us; the launch traced here: 226 us
  Pallas kernels  211 us (93%)
  local copies, waits for them, and re-layouts  9.7 us (4%)
  other arithmetic  4.34 us (2%)
    pallas_call x1, Pallas kernels, per_device(): pl.pallas_call(main_kernel, out_shape=(jax.ShapeDtypeStruct((ROWS, WIDTH)...  200 us
    pallas_call x1, Pallas kernels, per_device(): pl.pallas_call(prep_kernel, out_shape=(jax.ShapeDtypeStruct((64, 128), F3...  11 us

profile of v1, /device:TPU:33, one launch (start us, length us, event | category | flops | bytes accessed | tf_op | source)
XLA Modules:
  0.0 226.5 jit_solution(7636443167401171865)
XLA Ops:
  0.6 0.0 copy-start.1
  1.3 2.0 copy.13.head_ref
  3.3 2.0 copy.12.rel_ref
  5.4 0.0 copy-done.1
  5.4 1.4 copy.14.tail_ref
  6.7 11.0 %prep.1 = (f32[64,128]{1,0:T(8,128)}, s32[2048,1]{1,0:T(8,128)}) custom-call(s32[2048,1]{1,0:T(8,128)} %copy.12.rel_ref, s32[2048,1]{1,0:T(8,128)} %copy.13.head_ref, s32[2048,1]{1,0:T(8,128)} %copy.14.tail_ref), custom_call_target="tpu_custom_call" | custom-call | tf_op jit(solution)/shard_map/prep/pallas_call | solution.py:390
  17.8 200.1 %rescal.1 = (bf16[2048,512]{1,0:T(8,128)(2,1)}, f32[16,2048]{1,0:T(8,128)}, bf16[4,512,512]{2,1,0:T(8,128)(2,1)}, f32[4,4,8,128]{3,2,1,0:T(8,128)}) custom-call(s32[1]{0:T(128)S(6)} %copy.19.owner_ref, bf16[1024,512]{1,0:T(8,128)(2,1)} %ent_ref.1, f32[64,128]{1,0:T(8,128)} %get-tuple-element.10.table_ref, s32[2048,1]{1,0:T(8,128)} %get-tuple-element.11.pos_ref, ...), custom_call_target="tpu_custom_call" | custom-call | tf_op jit(solution)/shard_map/rescal/pallas_call | solution.py:429
  217.9 1.5 fusion
  219.3 0.9 slice_reduce_fusion
  220.2 0.6 copy.17
  220.8 0.0 copy-start
  220.8 4.3 %convert_element_type.8 = f32[4,512,512]{2,1,0:T(8,128)} convert(bf16[4,512,512]{2,1,0:T(8,128)(2,1)} %get-tuple-element.14) | non-fusion elementwise | flops 1048576 | bytes 6291456 | tf_op jit(solution)/shard_map/convert_element_type | solution.py:446
  225.1 0.0 copy-done
  225.1 1.3 copy.20
Async XLA Ops:
  0.6 4.7 %copy-start.1 = (s32[2048]{0:T(1024)S(1)}, s32[2048]{0:T(1024)}, u32[]{:S(2)}) copy-start(s32[2048]{0:T(1024)} %param.9) | copy-start | bytes 24580
  220.8 4.3 %copy-start = (bf16[2048,512]{1,0:T(8,128)(2,1)S(1)}, bf16[2048,512]{1,0:T(8,128)(2,1)}, u32[]{:S(2)}) copy-start(bf16[2048,512]{1,0:T(8,128)(2,1)} %get-tuple-element.21) | copy-start | bytes 6291460

commit v2 on v1

v2 whole, which is shorter than its diff:
```python
import jax
import jax.numpy as jnp
from jax import lax
from jax.experimental import pallas as pl
from jax.experimental.pallas import tpu as pltpu
from jax.sharding import PartitionSpec as P

MESH = pl.DeviceIdType.MESH
BF, F32, I32 = jnp.bfloat16, jnp.float32, jnp.int32
ROWS, WIDTH, NEG = 2048, 512, 1024
CHUNKS, SLOTS, CAP = 4, 32, 32
VMEM_BYTES = 61 * 2**20


def place():
    grp, rel = lax.axis_index("grp"), lax.axis_index("rel")
    x_hi, core = grp // 2, grp % 2
    x_lo, y, z = rel // 16, (rel // 4) % 4, rel % 4
    return x_hi, core, x_hi * 2 + x_lo, x_lo, y, z


def device_at(core, x, y, z):
    return ((x // 2) * 2 + core, (x % 2) * 16 + y * 4 + z)


def peer(j, d, sign, here):
    x_hi, core, x, x_lo, y, z = here
    dx, dm, odd = d % 2, d // 2, j % 2
    x = (x + dx * (1 + 2 * (x % 2) + 2 * (dm % 2))) % 4
    return device_at(core, x, (y + sign * dm * odd + 4) % 4, (z + sign * dm * (1 - odd) + 4) % 4)


def make_table(rel_ref, head_ref, tail_ref, table, pos, spots, here):
    x_hi, core, x, x_lo, y, z = here
    line = lax.broadcasted_iota(I32, (128, 128), 0)
    lane = lax.broadcasted_iota(I32, (128, 128), 1)
    earlier = jnp.where(line < lane, 1.0, 0.0).astype(BF)
    seen = jnp.zeros((128, 1), F32)
    total = jnp.zeros((128, 128), F32)
    for i in range(ROWS // 128):
        rel, head, tail = rel_ref[i : i + 1, :], head_ref[i : i + 1, :] + 1, tail_ref[i : i + 1, :] + 1
        hot = jnp.where(line == rel, 1.0, 0.0)
        before = jnp.dot(hot.astype(BF), earlier, preferred_element_type=F32) + seen
        rank = jnp.sum(hot * before, axis=0, keepdims=True).astype(I32)
        digit = jnp.where(line < 64, jnp.where(line < 32, head // 32, head % 32), jnp.where(line < 96, tail // 32, tail % 32))
        marks = jnp.where(line % 32 == rank, digit, 0).astype(F32).astype(BF)
        total = total + lax.dot_general(marks, hot.astype(BF), (((1,), (1,)), ((), ())), preferred_element_type=F32)
        seen = seen + jnp.sum(hot, axis=1, keepdims=True)
        owner = rel // 4
        dy, dz = (owner // 4 % 4 + 4 - y) % 4, (owner % 4 + 4 - z) % 4
        dx, odd = (owner // 16 + 2 - x_lo) % 2, rel % 2
        dm, dk = dy * odd + dz * (1 - odd), dz * odd + dy * (1 - odd)
        spot = (rel % 4) * (SLOTS * CAP) + (dk * 8 + dm * 2 + dx) * CAP + rank
        spots[i : i + 1, :] = spot
        pos[i * 128 : i * 128 + 128, :] = jnp.sum(jnp.where(line == lane, spot, 0), axis=1, keepdims=True)
    table[0:32, :] = total[0:32] * 32.0 + total[32:64] - 1.0
    table[32:64, :] = total[64:96] * 32.0 + total[96:128] - 1.0


def main_kernel(
    owner_ref, ent_ref, relation_ref, head_ref, tail_ref, accum_ref, weight_ref,
    grad_ref, loss_ref, new_ref, acc_out,
    table_ref, pos_ref, spots, rel_ref, acc_ref,
    out_rows, in_rows, out_back, in_back, out_loss, in_loss, w32, w16,
    own, g1s, g1r, gys, gyr, g2s, g2r,
    neg, n0s, n0r, n1, n1r, n2, n2r, n3, n3r, n4,
    w_sem, new_sem, rows_ss, rows_rs, back_ss, back_rs, loss_ss, loss_rs,
    wr_ss, wr_rs, wm_ss, wm_rs, g1_ss, g1_rs, gy_ss, gy_rs, neg_ss, neg_rs, grp_ss, grp_rs,
):
    here = place()
    x_hi, core, x, x_lo, y, z = here
    me = lax.axis_index("grp") * 32 + lax.axis_index("rel")
    mate = device_at(1 - core, x, y, z)
    across = device_at(core, (x + 2) % 4, y, z)
    beside = device_at(core, (x + 3 + 2 * (x % 2)) % 4, y, z)

    def remote(src, dst, ss, rs, device):
        return pltpu.make_async_remote_copy(src_ref=src, dst_ref=dst, send_sem=ss, recv_sem=rs, device_id=device, device_id_type=MESH)

    w_copy = pltpu.make_async_copy(weight_ref, w32, w_sem)
    w_copy.start()

    barrier = pltpu.get_barrier_semaphore()

    def greet(device):
        pl.semaphore_signal(barrier, inc=1, device_id=device, device_id_type=MESH)

    for d in range(1, 8):
        greet(peer(0, d, 1, here))
    for d in range(2, 8):
        greet(peer(1, d, 1, here))
    for device in (mate, across, beside):
        greet(device)
    out_loss[...] = jnp.zeros_like(out_loss)
    w_copy.wait()
    for j in range(2):
        w16[j, 0] = w32[j].astype(BF)
    pl.semaphore_wait(barrier, 16)

    mine = (owner_ref[0] == me).astype(F32).astype(BF)

    def ring(axis, d):
        if axis == 0:
            return device_at(core, (x + d) % 4, y, z), (x + d) % 4
        if axis == 1:
            return device_at(core, x, (y + d) % 4, z), (y + d) % 4
        return device_at(core, x, y, (z + d) % 4), (z + d) % 4

    def rows_of(start, size):
        return pl.ds(pl.multiple_of(start, size), size)

    block32 = core * 512 + x * 128 + y * 32

    def neg_copies(stage):
        if stage == 0:
            return [remote(n0s, n0r, neg_ss.at[0, 0], neg_rs.at[0, 0], mate)]
        if stage == 6:
            part = neg.at[rows_of(core * 512, 512)]
            return [remote(part, part, neg_ss.at[6, 0], neg_rs.at[6, 0], mate)]
        copies = []
        for d in (1, 2, 3):
            sems = neg_ss.at[stage, d - 1], neg_rs.at[stage, d - 1]
            device, there = ring({1: 0, 2: 1, 3: 2, 4: 1, 5: 0}[stage], d)
            if stage == 1:
                copies.append(remote(n1.at[rows_of(there * 128, 128)], n1r.at[d - 1], *sems, device))
            elif stage == 2:
                copies.append(remote(n2.at[rows_of(there * 32, 32)], n2r.at[d - 1], *sems, device))
            elif stage == 3:
                copies.append(remote(n3, n3r.at[d - 1], *sems, device))
            elif stage == 4:
                copies.append(remote(n4, neg.at[rows_of(block32, 32)], *sems, device))
            else:
                part = neg.at[rows_of(core * 512 + x * 128, 128)]
                copies.append(remote(part, part, *sems, device))
        return copies

    def neg_start(stage):
        if stage == 0:
            n0s[...] = ent_ref[rows_of((1 - core) * 512, 512), :] * mine
        elif stage == 1:
            n1[...] = ent_ref[rows_of(core * 512, 512), :] * mine + n0r[...]
        elif stage == 2:
            n2[...] = n1[rows_of(x * 128, 128), :] + n1r[0] + n1r[1] + n1r[2]
        elif stage == 3:
            n3[...] = n2[rows_of(y * 32, 32), :] + n2r[0] + n2r[1] + n2r[2]
        elif stage == 4:
            total = n3[...] + n3r[0] + n3r[1] + n3r[2]
            n4[...] = total
            neg[rows_of(block32, 32), :] = total
        for copy in neg_copies(stage):
            copy.start()

    def neg_wait(stage):
        for copy in neg_copies(stage):
            copy.wait()

    def rows_copy(j, n, sign):
        return remote(out_rows.at[j % 2, n], in_rows.at[j, n], rows_ss.at[j, n], rows_rs.at[j, n], peer(j, n % 8, sign, here))

    lane128 = lax.broadcasted_iota(I32, (64, 128), 1)
    lane1024 = lax.broadcasted_iota(I32, (64, NEG), 1).astype(F32)

    def send_rows(pair, i):
        j, odd = 2 * pair + i % 2, i % 2
        k = (i // 4 + pair) % 4
        first = k * 8 + (i // 2 % 2) * 4
        hots = []
        for m in range(4):
            d = (first + m) % 8
            dm = d // 2
            oy = (y + dm * odd + k * (1 - odd)) % 4
            oz = (z + dm * (1 - odd) + k * odd) % 4
            owner = ((x_lo + d) % 2) * 16 + oy * 4 + oz
            ids = jnp.sum(jnp.where(lane128 == owner * 4 + j, table_ref[...], 0.0), axis=1, keepdims=True)
            hots.append(jnp.where(lane1024 == ids, 1.0, 0.0).astype(BF))
        rows = jnp.dot(jnp.concatenate(hots, axis=0), ent_ref[...], preferred_element_type=F32).astype(BF)
        local = i // 2 % 2 == 0
        for m in range(4):
            if pair > 0:
                if m == 0:

                    @pl.when(jnp.logical_not(local))
                    def _():
                        rows_copy(j - 2, first, 1).wait_send()

                else:
                    rows_copy(j - 2, first + m, 1).wait_send()
        out_rows[j % 2, pl.ds(first, 4)] = rows.reshape(4, 64, WIDTH)
        for m in range(4):
            if m == 0:

                @pl.when(local)
                def _():
                    in_rows[j, first] = rows[0:64]

                @pl.when(jnp.logical_not(local))
                def _():
                    rows_copy(j, first, 1).start()

            else:
                rows_copy(j, first + m, 1).start()

    def send_steps(pair, first, last):
        def body(i, c):
            send_rows(pair, i)
            return c

        lax.fori_loop(first, last, body, 0)

    my_half = rows_of(core * 256, 256)

    def w_ring(j, k):
        device = device_at(core, x, (y + (4 - k) * (1 - j % 2)) % 4, (z + (4 - k) * (j % 2)) % 4)
        return remote(w16.at[j, 0, my_half], w16.at[j, k, my_half], wr_ss.at[j, k], wr_rs.at[j, k], device)

    def w_mate(j, k):
        part = w16.at[j, k, my_half]
        return remote(part, part, wm_ss.at[j, k], wm_rs.at[j, k], mate)

    def w_send(j):
        for k in (1, 2, 3):
            w_ring(j, k).start()

    def w_forward(j):
        for k in (1, 2, 3):
            w_ring(j, k).wait_recv()
            w_mate(j, k).start()

    w_send(0)
    w_send(1)
    neg_start(0)
    make_table(relation_ref, head_ref, tail_ref, table_ref, pos_ref, spots, here)
    at = 0
    for stage, to in enumerate((3, 6, 9, 12, 14, 16)):
        send_steps(0, at, to)
        at = to
        neg_wait(stage)
        neg_start(stage + 1)
    w_forward(0)
    w_forward(1)
    for j in (2, 3):
        w16[j, 0] = w32[j].astype(BF)
        w_send(j)
    send_steps(1, 0, 4)
    neg_wait(6)

    nt = (((1,), (1,)), ((), ()))
    tn = (((0,), (0,)), ((), ()))

    def back_copy(j, n, sign):
        return remote(out_back.at[j % 2, n], in_back.at[j, n], back_ss.at[j, n], back_rs.at[j, n], peer(j, n % 8, sign, here))

    def loss_copy(odd, d, sign):
        return remote(out_loss.at[odd, d // 4], in_loss.at[odd, d], loss_ss.at[odd, d], loss_rs.at[odd, d], peer(odd, d, sign, here))

    def score(j, i, c):
        k = (i + j // 2) % 4
        first = k * 8
        for d in range(1, 8):
            rows_copy(j, first + d, -1).wait_recv()
        slots = pl.ds(first, 8)
        h = in_rows[j, slots, 0:32, :].reshape(256, WIDTH)
        t = in_rows[j, slots, 32:64, :].reshape(256, WIDTH).astype(F32)
        w = w16.at[j, k]
        q = jnp.dot(h, w[...], preferred_element_type=F32).astype(BF)
        pos = jnp.sum(q.astype(F32) * t, axis=1, keepdims=True)
        s = lax.dot_general(q, neg[...], nt, preferred_element_type=F32)
        e = jnp.exp(-jnp.abs(s))
        soft = jnp.maximum(s, 0.0) + jnp.log1p(e)
        inv = 1.0 / (1.0 + e)
        coef = (jnp.where(s >= 0.0, inv, e * inv) * (1.0 / NEG)).astype(BF)
        g = jnp.dot(coef, neg[...], preferred_element_type=F32)
        ep = jnp.exp(-jnp.abs(pos))
        loss = jnp.maximum(-pos, 0.0) + jnp.log1p(ep) + jnp.sum(soft, axis=1, keepdims=True) * (1.0 / NEG)
        g = (g - jnp.where(pos <= 0.0, 1.0, ep) / (1.0 + ep) * t).astype(BF)
        back = lax.dot_general(g, w[...], nt, preferred_element_type=F32).astype(BF)
        if j >= 2:
            for d in range(1, 8):
                back_copy(j - 2, first + d, -1).wait_send()
        out_back[j % 2, slots] = back.reshape(8, CAP, WIDTH)
        for d in range(1, 8):
            back_copy(j, first + d, -1).start()
        in_back[j, first] = back[0:CAP]
        spot = lax.broadcasted_iota(I32, (256, 128), 1) == 0
        column = jnp.where(spot, loss, 0.0).astype(BF)
        row = lax.dot_general(jnp.ones((16, 128), BF), column, nt, preferred_element_type=F32).astype(BF)
        line = lax.broadcasted_iota(I32, (16, 128), 0) == (j // 2) * 4 + k
        for half in range(2):
            out_loss[j % 2, half] = jnp.where(line, row[:, half * 128 : half * 128 + 128], out_loss[j % 2, half])

        def outer(half):
            columns = pl.ds(pl.multiple_of(half * 256, 256), 256)
            return lax.dot_general(in_rows[j, slots, 0:32, columns].reshape(256, 256), g, tn, preferred_element_type=F32)

        if j >= 2:
            g1_copy(j - 2, k).wait_send()
        g1s[j % 2, k] = outer(1 - core).astype(BF)
        g1_copy(j, k).start()
        value = outer(core)

        @pl.when(k == 0)
        def _():
            own[j] = value

        @pl.when(k > 0)
        def _():
            if j >= 2:
                gy_copy(j - 2, k).wait_send()
            gys[j % 2, k] = value.astype(BF)

        @pl.when(i > 0)
        def _():
            g1_finish(j, (i - 1 + j // 2) % 4)

        return c

    def g1_copy(j, k):
        return remote(g1s.at[j % 2, k], g1r.at[j, k], g1_ss.at[j, k], g1_rs.at[j, k], mate)

    def gy_copy(j, k):
        device = device_at(core, x, (y + k * (1 - j % 2)) % 4, (z + k * (j % 2)) % 4)
        return remote(gys.at[j % 2, k], gyr.at[j, k], gy_ss.at[j, k], gy_rs.at[j, k], device)

    def g1_finish(j, k):
        g1_copy(j, k).wait_recv()

        @pl.when(k == 0)
        def _():
            own[j] = own[j] + g1r[j, 0].astype(F32)

        @pl.when(k > 0)
        def _():
            gys[j % 2, k] = (gys[j % 2, k].astype(F32) + g1r[j, k].astype(F32)).astype(BF)
            gy_copy(j, k).start()

    def gy_finish(j):
        for k in (1, 2, 3):
            gy_copy(j, k).wait_recv()
        own[j] = own[j] + gyr[j, 1].astype(F32) + gyr[j, 2].astype(F32) + gyr[j, 3].astype(F32)
        g2s[j] = own[j].astype(BF)
        g2_copy(j).start()

    def g2_copy(j):
        return remote(g2s.at[j], g2r.at[j], grp_ss.at[1, j], grp_rs.at[1, j], across)

    def g4_copies(j):
        part = rel_ref.at[j, rows_of(core * 256, 256)]
        tile = acc_ref.at[j, pl.ds(core * 2, 2)]
        return (
            remote(part, part, grp_ss.at[4, j], grp_rs.at[4, j], mate),
            remote(tile, tile, grp_ss.at[5, j], grp_rs.at[5, j], mate),
        )

    def g2_finish(j):
        g2_copy(j).wait_recv()
        eye = lax.broadcasted_iota(I32, (128, 128), 0) == lax.broadcasted_iota(I32, (128, 128), 1)
        for part in range(2):
            here_rows = slice(part * 128, part * 128 + 128)
            total = g2s[j, here_rows, :].astype(F32) + g2r[j, here_rows, :].astype(F32)
            quarter = core * 2 + part
            before = accum_ref[j : j + 1, pl.ds(pl.multiple_of(quarter * 128, 128), 128)]
            before = jnp.sum(jnp.where(eye, before, 0.0), axis=1, keepdims=True)
            after = before + jnp.sum(total * total, axis=1, keepdims=True) * (1.0 / WIDTH)
            rows = rows_of(quarter * 128, 128)
            rel_ref[j, rows, :] = (w32[j, rows, :] - total / jnp.sqrt(after)).astype(BF)
            line = jnp.sum(jnp.where(eye, after, 0.0), axis=0, keepdims=True)
            acc_ref[j, quarter] = jnp.broadcast_to(line, (8, 128))
        for copy in g4_copies(j):
            copy.start()

    def collect_wait(j):
        for n in range(SLOTS):
            if n % 8 > 0:
                back_copy(j, n, 1).wait_recv()

    def collect(j, first, last):
        def block(i, c):
            rows = pl.ds(pl.multiple_of(i * 256, 256), 256)
            slot = lax.broadcasted_iota(I32, (256, SLOTS * CAP), 1) + j * (SLOTS * CAP)
            pick = jnp.where(pos_ref[rows, :] == slot, 1.0, 0.0).astype(BF)
            stack = in_back[j].reshape(SLOTS * CAP, WIDTH)
            part = jnp.dot(pick, stack, preferred_element_type=F32).astype(BF)
            if j == 0:
                grad_ref[rows, :] = part
            else:
                grad_ref[rows, :] = grad_ref[rows, :] + part
            return c

        lax.fori_loop(first, last, block, 0)

    def send_losses():
        for odd in range(2):
            in_loss[odd, 0] = out_loss[odd, 0]
            for d in range(1, 8):
                loss_copy(odd, d, -1).start()

    def collect_losses():
        group = lax.broadcasted_iota(I32, (16, 128), 1) // CAP
        tiles = []
        for odd in range(2):
            for half in range(2):
                value = jnp.zeros((16, 128), F32)
                for m in range(4):
                    if half + m > 0:
                        loss_copy(odd, half * 4 + m, 1).wait_recv()
                    value = jnp.where(group == m, in_loss[odd, half * 4 + m].astype(F32), value)
                tiles.append(value)
        stack = jnp.concatenate(tiles, axis=0).astype(BF)
        line = lax.broadcasted_iota(I32, (64, 128), 0)
        full = lax.broadcasted_iota(I32, (128, 128), 0)
        for i in range(ROWS // 128):
            spot = spots[i : i + 1, :]
            j = spot // 1024
            row = (j % 2) * 32 + (spot // 128 % 2) * 16 + (j // 2) * 4 + spot // 256 % 4
            pick = jnp.where(line == row, 1.0, 0.0).astype(BF)
            found = lax.dot_general(stack, pick, tn, preferred_element_type=F32)
            loss_ref[i : i + 1, :] = jnp.sum(jnp.where(full == spot % 128, found, 0.0), axis=0, keepdims=True)

    def g4_finish(j):
        for copy in g4_copies(j):
            copy.wait_recv()
        for q in range(4):
            acc_out[j : j + 1, q * 128 : q * 128 + 128] = acc_ref[j, q, 0:1]
        w32[j] = rel_ref[j].astype(F32)
        pltpu.make_async_copy(w32.at[j], new_ref.at[j], new_sem.at[j]).start()

    for j in range(CHUNKS):
        for k in (1, 2, 3):
            w_mate(j, k).wait_recv()
        if j == 0:

            def mixed(i, c):
                score(0, i, c)

                @pl.when(i < 3)
                def _():
                    send_steps(1, i * 4 + 4, i * 4 + 8)

                return c

            lax.fori_loop(0, 4, mixed, 0)
            w_forward(2)
            w_forward(3)
        else:
            lax.fori_loop(0, 4, lambda i, c, j=j: score(j, i, c), 0)
        if j == CHUNKS - 1:
            send_losses()
        g1_finish(j, (3 + j // 2) % 4)
        if j >= 1:
            gy_finish(j - 1)
        if j >= 2:
            g2_finish(j - 2)
        if j >= 3:
            g4_finish(j - 3)
        if j >= 1:
            collect_wait(j - 1)
            collect(j - 1, 0, 8)
    g2_finish(2)
    g4_finish(1)
    gy_finish(3)
    collect_wait(3)
    collect(3, 0, 4)
    g2_finish(3)
    g4_finish(2)
    collect(3, 4, 8)
    collect_losses()
    g4_finish(3)

    for j in range(CHUNKS):
        for k in (1, 2, 3):
            w_ring(j, k).wait_send()
            w_mate(j, k).wait_send()
        if j >= 2:
            for n in range(SLOTS):
                if n % 8 > 0:
                    rows_copy(j, n, 1).wait_send()
                    back_copy(j, n, -1).wait_send()
            for k in range(4):
                g1_copy(j, k).wait_send()
            for k in (1, 2, 3):
                gy_copy(j, k).wait_send()
        for copy in (g2_copy(j), *g4_copies(j)):
            copy.wait_send()
        pltpu.make_async_copy(w32.at[j], new_ref.at[j], new_sem.at[j]).wait()
    for odd in range(2):
        for d in range(1, 8):
            loss_copy(odd, d, -1).wait_send()


def per_device(head_ids, relations, tail_ids, neg_owner, entities, rel_weight, rel_accum):
    vmem, anywhere = pl.BlockSpec(memory_space=pltpu.VMEM), pl.BlockSpec(memory_space=pl.ANY)
    tiles = (ROWS // 128, 128)
    dma = pltpu.SemaphoreType.DMA
    scratch = [
        pltpu.VMEM((64, 128), F32),
        pltpu.VMEM((ROWS, 1), I32),
        pltpu.VMEM((16, 128), I32),
        pltpu.VMEM((CHUNKS, WIDTH, WIDTH), BF),
        pltpu.VMEM((CHUNKS, 4, 8, 128), F32),
        pltpu.VMEM((2, SLOTS, 64, WIDTH), BF),
        pltpu.VMEM((CHUNKS, SLOTS, 64, WIDTH), BF),
        pltpu.VMEM((2, SLOTS, CAP, WIDTH), BF),
        pltpu.VMEM((CHUNKS, SLOTS, CAP, WIDTH), BF),
        pltpu.VMEM((2, 2, 16, 128), BF),
        pltpu.VMEM((2, 8, 16, 128), BF),
        pltpu.VMEM((CHUNKS, WIDTH, WIDTH), F32),
        pltpu.VMEM((CHUNKS, 4, WIDTH, WIDTH), BF),
        pltpu.VMEM((CHUNKS, 256, WIDTH), F32),
        pltpu.VMEM((2, 4, 256, WIDTH), BF),
        pltpu.VMEM((CHUNKS, 4, 256, WIDTH), BF),
        pltpu.VMEM((2, 4, 256, WIDTH), BF),
        pltpu.VMEM((CHUNKS, 4, 256, WIDTH), BF),
        pltpu.VMEM((CHUNKS, 256, WIDTH), BF),
        pltpu.VMEM((CHUNKS, 256, WIDTH), BF),
        pltpu.VMEM((NEG, WIDTH), BF),
        pltpu.VMEM((512, WIDTH), BF),
        pltpu.VMEM((512, WIDTH), BF),
        pltpu.VMEM((512, WIDTH), BF),
        pltpu.VMEM((3, 128, WIDTH), BF),
        pltpu.VMEM((128, WIDTH), BF),
        pltpu.VMEM((3, 32, WIDTH), BF),
        pltpu.VMEM((32, WIDTH), BF),
        pltpu.VMEM((3, 32, WIDTH), BF),
        pltpu.VMEM((32, WIDTH), BF),
        dma,
        dma((CHUNKS,)),
        *[dma((CHUNKS, SLOTS))] * 4,
        *[dma((2, 8))] * 2,
        *[dma((CHUNKS, 4))] * 8,
        *[dma((7, 3))] * 2,
        *[dma((6, CHUNKS))] * 2,
    ]
    head_grad, losses, new_rel, new_accum = pl.pallas_call(
        main_kernel,
        out_shape=(
            jax.ShapeDtypeStruct((ROWS, WIDTH), BF),
            jax.ShapeDtypeStruct((16, 128), F32),
            jax.ShapeDtypeStruct((CHUNKS, WIDTH, WIDTH), F32),
            jax.ShapeDtypeStruct((CHUNKS, WIDTH), F32),
        ),
        in_specs=[pl.BlockSpec(memory_space=pltpu.SMEM), *[vmem] * 5, anywhere],
        out_specs=(vmem, vmem, anywhere, vmem),
        scratch_shapes=scratch,
        compiler_params=pltpu.CompilerParams(collective_id=0, has_side_effects=True, vmem_limit_bytes=VMEM_BYTES),
        name="rescal",
    )(neg_owner, entities, relations.reshape(tiles), head_ids.reshape(tiles), tail_ids.reshape(tiles), rel_accum, rel_weight)
    return losses.reshape(ROWS).astype(BF), head_grad, new_rel, new_accum


def solution(mesh):
    placed = (
        P(("grp", "rel")),
        P(("grp", "rel"), None),
        P(("grp", "rel")),
        P(),
        P(("grp", "rel"), None),
        P("rel", None, None),
        P("rel", None),
    )
    return jax.shard_map(
        per_device,
        mesh=mesh,
        in_specs=placed,
        out_specs=(
            P(("grp", "rel")),
            P(("grp", "rel"), None),
            P("rel", None, None),
            P("rel", None),
        ),
        check_vma=False,
    )
```

time: 227 us -> 179 us (0.79)
  Pallas kernels: 211 us -> 169 us
  local copies, waits for them, and re-layouts: 9.7 us -> 5.66 us
  other arithmetic: 4.34 us -> 1.44 us
    pallas_call x1, Pallas kernels: 200 us -> 169 us  [per_device(): pl.pallas_call(main_kernel, out_shape=(jax.ShapeDtypeStruct((ROWS, WIDTH)...]
    pallas_call x1 -> x0, Pallas kernels: 11 us -> none  [per_device(): pl.pallas_call(prep_kernel, out_shape=(jax.ShapeDtypeStruct((64, 128), F3...]
    reshape x2 -> x0, local copies, waits for them, and re-layouts: 3.4 us -> none  [the longest x1 2.04 us: per_device(): head_ids.reshape(ROWS, 1)]
    convert_element_type x1, other arithmetic: 4.34 us -> 1.44 us  [per_device(): return (losses.reshape(ROWS).astype(BF), head_grad, new_rel, new_accum)]
    slice x2 -> x0, local copies, waits for them, and re-layouts: 2.33 us -> none  [the longest x1 1.46 us: per_device(): losses[0].astype(BF)]
where the time goes in v2:
time: 179 us; the launch traced here: 177 us
  Pallas kernels  169 us (94%)
  local copies, waits for them, and re-layouts  5.66 us (3%)
    pallas_call x1, Pallas kernels, per_device(): pl.pallas_call(main_kernel, out_shape=(jax.ShapeDtypeStruct((ROWS, WIDTH)...  169 us
    unnamed x7, local copies, waits for them, and re-layouts  5.66 us

profile of v2, /device:TPU:33, one launch (start us, length us, event | category | flops | bytes accessed | tf_op | source)
XLA Modules:
  0.0 177.4 jit_solution(11213955738468827239)
XLA Ops:
  1.3 169.0 %rescal.1 = (bf16[2048,512]{1,0:T(8,128)(2,1)}, f32[16,128]{1,0:T(8,128)}, f32[4,512,512]{2,1,0:T(8,128)}, f32[4,512]{1,0:T(4,128)}) custom-call(s32[1]{0:T(128)S(6)} %copy.14.owner_ref, bf16[1024,512]{1,0:T(8,128)(2,1)} %ent_ref.1, s32[16,128]{1,0:T(8,128)} %bitcast.5, s32[16,128]{1,0:T(8,128)} %bitcast.6, s32[16,128]{1,0:T(8,128)} %bitcast.7, ...), custom_call_target="tpu_custom_call" | custom-call | tf_op jit(solution)/shard_map/rescal/pallas_call | solution.py:533
  170.3 0.0 copy-start
  170.3 1.4 convert_bitcast_fusion
  171.7 3.0 %copy.15 = bf16[2048,512]{1,0:T(8,128)(2,1)} copy(bf16[2048,512]{1,0:T(8,128)(2,1)} %get-tuple-element.17) | data formatting | bytes 4194304
  174.8 0.0 copy-done
  174.8 0.0 copy-start.1
  174.8 2.0 %copy.16 = f32[4,512,512]{2,1,0:T(8,128)} copy(f32[4,512,512]{2,1,0:T(8,128)S(1)} %copy-done) | data formatting | bytes 8388608
  176.8 0.0 copy-done.1
  176.8 0.6 copy.17
Async XLA Ops:
  170.3 4.5 %copy-start = (f32[4,512,512]{2,1,0:T(8,128)S(1)}, f32[4,512,512]{2,1,0:T(8,128)}, u32[]{:S(2)}) copy-start(f32[4,512,512]{2,1,0:T(8,128)} %get-tuple-element.18) | copy-start | bytes 12582916
  174.8 2.0 %copy-start.1 = (f32[4,512]{1,0:T(4,128)S(1)}, f32[4,512]{1,0:T(4,128)}, u32[]{:S(2)}) copy-start(f32[4,512]{1,0:T(4,128)} %get-tuple-element.19) | copy-start | bytes 24580

commit v3 on v2

--- a/solution.py
+++ b/solution.py
@@ -59,12 +59,12 @@
 
 def main_kernel(
     owner_ref, ent_ref, relation_ref, head_ref, tail_ref, accum_ref, weight_ref,
-    grad_ref, loss_ref, new_ref, acc_out,
-    table_ref, pos_ref, spots, rel_ref, acc_ref,
+    grad_out, loss_ref, new_ref, acc_out,
+    grad_ref,    table_ref, pos_ref, spots, rel_ref, acc_ref,
     out_rows, in_rows, out_back, in_back, out_loss, in_loss, w32, w16,
     own, g1s, g1r, gys, gyr, g2s, g2r,
     neg, n0s, n0r, n1, n1r, n2, n2r, n3, n3r, n4,
-    w_sem, new_sem, rows_ss, rows_rs, back_ss, back_rs, loss_ss, loss_rs,
+    w_sem, new_sem, grad_sem, rows_ss, rows_rs, back_ss, back_rs, loss_ss, loss_rs,
     wr_ss, wr_rs, wm_ss, wm_rs, g1_ss, g1_rs, gy_ss, gy_rs, neg_ss, neg_rs, grp_ss, grp_rs,
 ):
     here = place()
@@ -77,8 +77,9 @@
     def remote(src, dst, ss, rs, device):
         return pltpu.make_async_remote_copy(src_ref=src, dst_ref=dst, send_sem=ss, recv_sem=rs, device_id=device, device_id_type=MESH)
 
-    w_copy = pltpu.make_async_copy(weight_ref, w32, w_sem)
-    w_copy.start()
+    w_copies = [pltpu.make_async_copy(weight_ref.at[j], w32.at[j], w_sem.at[j]) for j in range(CHUNKS)]
+    for copy in w_copies:
+        copy.start()
 
     barrier = pltpu.get_barrier_semaphore()
 
@@ -92,8 +93,8 @@
     for device in (mate, across, beside):
         greet(device)
     out_loss[...] = jnp.zeros_like(out_loss)
-    w_copy.wait()
     for j in range(2):
+        w_copies[j].wait()
         w16[j, 0] = w32[j].astype(BF)
     pl.semaphore_wait(barrier, 16)
 
@@ -162,7 +163,7 @@
 
     def send_rows(pair, i):
         j, odd = 2 * pair + i % 2, i % 2
-        k = (i // 4 + pair) % 4
+        k = (i // 4 + 2 * pair) % 4
         first = k * 8 + (i // 2 % 2) * 4
         hots = []
         for m in range(4):
@@ -217,28 +218,45 @@
         part = w16.at[j, k, my_half]
         return remote(part, part, wm_ss.at[j, k], wm_rs.at[j, k], mate)
 
+    def w_relay(j, k):
+        part = rows_of(core * 256 + (k // 2) * 128, 128)
+        device = device_at(core, x, (y + (4 - k) * (1 - j % 2)) % 4, (z + (4 - k) * (j % 2)) % 4)
+        return remote(w16.at[j, k, part], w16.at[j, 2, part], wr_ss.at[j, k - 1], wr_rs.at[j, k - 1], device)
+
     def w_send(j):
-        for k in (1, 2, 3):
+        for k in (1, 3):
             w_ring(j, k).start()
 
+    def w_pass(j):
+        for k in (1, 3):
+            w_ring(j, k).wait_recv()
+            w_relay(j, k).start()
+            w_mate(j, k).start()
+
     def w_forward(j):
-        for k in (1, 2, 3):
-            w_ring(j, k).wait_recv()
-            w_mate(j, k).start()
-
+        for k in (1, 3):
+            w_relay(j, k).wait_recv()
+        w_mate(j, 2).start()
+
+    neg_start(0)
     w_send(0)
     w_send(1)
-    neg_start(0)
+    neg_wait(0)
+    neg_start(1)
     make_table(relation_ref, head_ref, tail_ref, table_ref, pos_ref, spots, here)
     at = 0
-    for stage, to in enumerate((3, 6, 9, 12, 14, 16)):
+    for stage, to in ((1, 3), (2, 6), (3, 9), (4, 12), (5, 16)):
         send_steps(0, at, to)
         at = to
         neg_wait(stage)
         neg_start(stage + 1)
+        if stage == 3:
+            w_pass(0)
+            w_pass(1)
     w_forward(0)
     w_forward(1)
     for j in (2, 3):
+        w_copies[j].wait()
         w16[j, 0] = w32[j].astype(BF)
         w_send(j)
     send_steps(1, 0, 4)
@@ -254,7 +272,7 @@
         return remote(out_loss.at[odd, d // 4], in_loss.at[odd, d], loss_ss.at[odd, d], loss_rs.at[odd, d], peer(odd, d, sign, here))
 
     def score(j, i, c):
-        k = (i + j // 2) % 4
+        k = (i + j // 2 * 2) % 4
         first = k * 8
         for d in range(1, 8):
             rows_copy(j, first + d, -1).wait_recv()
@@ -310,7 +328,7 @@
 
         @pl.when(i > 0)
         def _():
-            g1_finish(j, (i - 1 + j // 2) % 4)
+            g1_finish(j, (i - 1 + j // 2 * 2) % 4)
 
         return c
 
@@ -368,22 +386,28 @@
         for copy in g4_copies(j):
             copy.start()
 
-    def collect_wait(j):
-        for n in range(SLOTS):
+    def collect_wait(j, low, high):
+        for n in range(low, high):
             if n % 8 > 0:
                 back_copy(j, n, 1).wait_recv()
 
-    def collect(j, first, last):
+    def grad_copy(i):
+        rows = rows_of(i * 256, 256)
+        return pltpu.make_async_copy(grad_ref.at[rows], grad_out.at[rows], grad_sem.at[i])
+
+    def collect(j, low, high, first=0, last=8, final=False):
         def block(i, c):
             rows = pl.ds(pl.multiple_of(i * 256, 256), 256)
-            slot = lax.broadcasted_iota(I32, (256, SLOTS * CAP), 1) + j * (SLOTS * CAP)
+            slot = lax.broadcasted_iota(I32, (256, (high - low) * CAP), 1) + (j * SLOTS + low) * CAP
             pick = jnp.where(pos_ref[rows, :] == slot, 1.0, 0.0).astype(BF)
-            stack = in_back[j].reshape(SLOTS * CAP, WIDTH)
+            stack = in_back[j, low:high].reshape((high - low) * CAP, WIDTH)
             part = jnp.dot(pick, stack, preferred_element_type=F32).astype(BF)
             if j == 0:
                 grad_ref[rows, :] = part
             else:
                 grad_ref[rows, :] = grad_ref[rows, :] + part
+            if final:
+                grad_copy(i).start()
             return c
 
         lax.fori_loop(first, last, block, 0)
@@ -439,13 +463,16 @@
                 return c
 
             lax.fori_loop(0, 4, mixed, 0)
+            w_pass(2)
+            w_pass(3)
+        else:
+            lax.fori_loop(0, 4, lambda i, c, j=j: score(j, i, c), 0)
+        if j == 1:
             w_forward(2)
             w_forward(3)
-        else:
-            lax.fori_loop(0, 4, lambda i, c, j=j: score(j, i, c), 0)
         if j == CHUNKS - 1:
             send_losses()
-        g1_finish(j, (3 + j // 2) % 4)
+        g1_finish(j, (3 + j // 2 * 2) % 4)
         if j >= 1:
             gy_finish(j - 1)
         if j >= 2:
@@ -453,23 +480,27 @@
         if j >= 3:
             g4_finish(j - 3)
         if j >= 1:
-            collect_wait(j - 1)
-            collect(j - 1, 0, 8)
+            collect_wait(j - 1, 0, SLOTS)
+            collect(j - 1, 0, SLOTS)
     g2_finish(2)
     g4_finish(1)
+    collect_wait(3, 16, 32)
+    collect(3, 16, 32)
     gy_finish(3)
-    collect_wait(3)
-    collect(3, 0, 4)
+    collect_wait(3, 0, 16)
+    collect(3, 0, 16, 0, 4, final=True)
     g2_finish(3)
     g4_finish(2)
-    collect(3, 4, 8)
+    collect(3, 0, 16, 4, 8, final=True)
     collect_losses()
     g4_finish(3)
 
     for j in range(CHUNKS):
         for k in (1, 2, 3):
+            w_mate(j, k).wait_send()
+        for k in (1, 3):
             w_ring(j, k).wait_send()
-            w_mate(j, k).wait_send()
+            w_relay(j, k).wait_send()
         if j >= 2:
             for n in range(SLOTS):
                 if n % 8 > 0:
@@ -485,6 +516,8 @@
     for odd in range(2):
         for d in range(1, 8):
             loss_copy(odd, d, -1).wait_send()
+    for i in range(8):
+        grad_copy(i).wait()
 
 
 def per_device(head_ids, relations, tail_ids, neg_owner, entities, rel_weight, rel_accum):
@@ -492,6 +525,7 @@
     tiles = (ROWS // 128, 128)
     dma = pltpu.SemaphoreType.DMA
     scratch = [
+        pltpu.VMEM((ROWS, WIDTH), BF),
         pltpu.VMEM((64, 128), F32),
         pltpu.VMEM((ROWS, 1), I32),
         pltpu.VMEM((16, 128), I32),
@@ -522,8 +556,9 @@
         pltpu.VMEM((32, WIDTH), BF),
         pltpu.VMEM((3, 32, WIDTH), BF),
         pltpu.VMEM((32, WIDTH), BF),
-        dma,
         dma((CHUNKS,)),
+        dma((CHUNKS,)),
+        dma((8,)),
         *[dma((CHUNKS, SLOTS))] * 4,
         *[dma((2, 8))] * 2,
         *[dma((CHUNKS, 4))] * 8,
@@ -539,7 +574,7 @@
             jax.ShapeDtypeStruct((CHUNKS, WIDTH), F32),
         ),
         in_specs=[pl.BlockSpec(memory_space=pltpu.SMEM), *[vmem] * 5, anywhere],
-        out_specs=(vmem, vmem, anywhere, vmem),
+        out_specs=(anywhere, vmem, anywhere, vmem),
         scratch_shapes=scratch,
         compiler_params=pltpu.CompilerParams(collective_id=0, has_side_effects=True, vmem_limit_bytes=VMEM_BYTES),
         name="rescal",

time: 179 us -> 170 us (0.950)
  Pallas kernels: 169 us -> 159 us
    pallas_call x1, Pallas kernels: 169 us -> 159 us  [per_device(): pl.pallas_call(main_kernel, out_shape=(jax.ShapeDtypeStruct((ROWS, WIDTH)...]
where the time goes in v3:
time: 170 us; the launch traced here: 167 us
  Pallas kernels  159 us (94%)
  local copies, waits for them, and re-layouts  5.66 us (3%)
    pallas_call x1, Pallas kernels, per_device(): pl.pallas_call(main_kernel, out_shape=(jax.ShapeDtypeStruct((ROWS, WIDTH)...  159 us
    unnamed x7, local copies, waits for them, and re-layouts  5.66 us

profile of v3, /device:TPU:33, one launch (start us, length us, event | category | flops | bytes accessed | tf_op | source)
XLA Modules:
  0.0 167.0 jit_solution(9149756758609888837)
XLA Ops:
  1.3 158.6 %rescal.1 = (bf16[2048,512]{1,0:T(8,128)(2,1)}, f32[16,128]{1,0:T(8,128)}, f32[4,512,512]{2,1,0:T(8,128)}, f32[4,512]{1,0:T(4,128)}) custom-call(s32[1]{0:T(128)S(6)} %copy.14.owner_ref, bf16[1024,512]{1,0:T(8,128)(2,1)} %ent_ref.1, s32[16,128]{1,0:T(8,128)} %bitcast.5, s32[16,128]{1,0:T(8,128)} %bitcast.6, s32[16,128]{1,0:T(8,128)} %bitcast.7, ...), custom_call_target="tpu_custom_call" | custom-call | tf_op jit(solution)/shard_map/rescal/pallas_call | solution.py:568
  159.9 0.0 copy-start
  159.9 1.4 convert_bitcast_fusion
  161.3 3.0 %copy.15 = bf16[2048,512]{1,0:T(8,128)(2,1)} copy(bf16[2048,512]{1,0:T(8,128)(2,1)} %get-tuple-element.17) | data formatting | bytes 4194304
  164.4 0.0 copy-done
  164.4 0.0 copy-start.1
  164.4 2.0 %copy.16 = f32[4,512,512]{2,1,0:T(8,128)} copy(f32[4,512,512]{2,1,0:T(8,128)S(1)} %copy-done) | data formatting | bytes 8388608
  166.4 0.0 copy-done.1
  166.4 0.6 copy.17
Async XLA Ops:
  159.9 4.5 %copy-start = (f32[4,512,512]{2,1,0:T(8,128)S(1)}, f32[4,512,512]{2,1,0:T(8,128)}, u32[]{:S(2)}) copy-start(f32[4,512,512]{2,1,0:T(8,128)} %get-tuple-element.18) | copy-start | bytes 12582916
  164.4 2.0 %copy-start.1 = (f32[4,512]{1,0:T(4,128)S(1)}, f32[4,512]{1,0:T(4,128)}, u32[]{:S(2)}) copy-start(f32[4,512]{1,0:T(4,128)} %get-tuple-element.19) | copy-start | bytes 24580

commit v4 on v3

--- a/solution.py
+++ b/solution.py
@@ -323,7 +323,16 @@
         @pl.when(k > 0)
         def _():
             if j >= 2:
-                gy_copy(j - 2, k).wait_send()
+
+                @pl.when(k == 2)
+                def _():
+                    gz_copy(j - 2, 1).wait_send()
+                    gz_copy(j - 2, 3).wait_send()
+
+                @pl.when(k != 2)
+                def _():
+                    gy_copy(j - 2, k).wait_send()
+
             gys[j % 2, k] = value.astype(BF)
 
         @pl.when(i > 0)
@@ -339,6 +348,18 @@
         device = device_at(core, x, (y + k * (1 - j % 2)) % 4, (z + k * (j % 2)) % 4)
         return remote(gys.at[j % 2, k], gyr.at[j, k], gy_ss.at[j, k], gy_rs.at[j, k], device)
 
+    def gz_copy(j, k):
+        device = device_at(core, x, (y + k * (1 - j % 2)) % 4, (z + k * (j % 2)) % 4)
+        half = pl.ds((k // 2) * 128, 128)
+        return remote(gys.at[j % 2, 2, half], gyr.at[j, k - 1, pl.ds(0, 128)], gy_ss.at[j, k - 1], gy_rs.at[j, k - 1], device)
+
+    def gz_finish(j):
+        for k in (1, 3):
+            gz_copy(j, k).wait_recv()
+            half = slice((k // 2) * 128, (k // 2) * 128 + 128)
+            gys[j % 2, k, half, :] = (gys[j % 2, k, half, :].astype(F32) + gyr[j, k - 1, 0:128, :].astype(F32)).astype(BF)
+            gy_copy(j, k).start()
+
     def g1_finish(j, k):
         g1_copy(j, k).wait_recv()
 
@@ -349,12 +370,16 @@
         @pl.when(k > 0)
         def _():
             gys[j % 2, k] = (gys[j % 2, k].astype(F32) + g1r[j, k].astype(F32)).astype(BF)
-            gy_copy(j, k).start()
+
+        @pl.when(k == 2)
+        def _():
+            gz_copy(j, 1).start()
+            gz_copy(j, 3).start()
 
     def gy_finish(j):
-        for k in (1, 2, 3):
+        for k in (1, 3):
             gy_copy(j, k).wait_recv()
-        own[j] = own[j] + gyr[j, 1].astype(F32) + gyr[j, 2].astype(F32) + gyr[j, 3].astype(F32)
+        own[j] = own[j] + gyr[j, 1].astype(F32) + gyr[j, 3].astype(F32)
         g2s[j] = own[j].astype(BF)
         g2_copy(j).start()
 
@@ -473,6 +498,8 @@
         if j == CHUNKS - 1:
             send_losses()
         g1_finish(j, (3 + j // 2 * 2) % 4)
+        if j == CHUNKS - 1:
+            gz_finish(j)
         if j >= 1:
             gy_finish(j - 1)
         if j >= 2:
@@ -482,6 +509,8 @@
         if j >= 1:
             collect_wait(j - 1, 0, SLOTS)
             collect(j - 1, 0, SLOTS)
+        if j < CHUNKS - 1:
+            gz_finish(j)
     g2_finish(2)
     g4_finish(1)
     collect_wait(3, 16, 32)
@@ -508,8 +537,9 @@
                     back_copy(j, n, -1).wait_send()
             for k in range(4):
                 g1_copy(j, k).wait_send()
-            for k in (1, 2, 3):
+            for k in (1, 3):
                 gy_copy(j, k).wait_send()
+                gz_copy(j, k).wait_send()
         for copy in (g2_copy(j), *g4_copies(j)):
             copy.wait_send()
         pltpu.make_async_copy(w32.at[j], new_ref.at[j], new_sem.at[j]).wait()

time: 170 us -> 170 us (level)
  no operation moved by 1% of the time
where the time goes in v4:
time: 170 us; the launch traced here: 167 us
  Pallas kernels  159 us (94%)
  local copies, waits for them, and re-layouts  5.66 us (3%)
    pallas_call x1, Pallas kernels, per_device(): pl.pallas_call(main_kernel, out_shape=(jax.ShapeDtypeStruct((ROWS, WIDTH)...  159 us
    unnamed x7, local copies, waits for them, and re-layouts  5.66 us

profile of v4, /device:TPU:33, one launch (start us, length us, event | category | flops | bytes accessed | tf_op | source)
XLA Modules:
  0.0 167.5 jit_solution(6488268197649758277)
XLA Ops:
  1.3 159.1 %rescal.1 = (bf16[2048,512]{1,0:T(8,128)(2,1)}, f32[16,128]{1,0:T(8,128)}, f32[4,512,512]{2,1,0:T(8,128)}, f32[4,512]{1,0:T(4,128)}) custom-call(s32[1]{0:T(128)S(6)} %copy.14.owner_ref, bf16[1024,512]{1,0:T(8,128)(2,1)} %ent_ref.1, s32[16,128]{1,0:T(8,128)} %bitcast.5, s32[16,128]{1,0:T(8,128)} %bitcast.6, s32[16,128]{1,0:T(8,128)} %bitcast.7, ...), custom_call_target="tpu_custom_call" | custom-call | tf_op jit(solution)/shard_map/rescal/pallas_call | solution.py:598
  160.4 0.0 copy-start
  160.4 1.4 convert_bitcast_fusion
  161.8 3.0 %copy.15 = bf16[2048,512]{1,0:T(8,128)(2,1)} copy(bf16[2048,512]{1,0:T(8,128)(2,1)} %get-tuple-element.17) | data formatting | bytes 4194304
  164.9 0.0 copy-done
  164.9 0.0 copy-start.1
  164.9 2.0 %copy.16 = f32[4,512,512]{2,1,0:T(8,128)} copy(f32[4,512,512]{2,1,0:T(8,128)S(1)} %copy-done) | data formatting | bytes 8388608
  166.9 0.0 copy-done.1
  166.9 0.6 copy.17
Async XLA Ops:
  160.4 4.5 %copy-start = (f32[4,512,512]{2,1,0:T(8,128)S(1)}, f32[4,512,512]{2,1,0:T(8,128)}, u32[]{:S(2)}) copy-start(f32[4,512,512]{2,1,0:T(8,128)} %get-tuple-element.18) | copy-start | bytes 12582916
  164.9 2.0 %copy-start.1 = (f32[4,512]{1,0:T(4,128)S(1)}, f32[4,512]{1,0:T(4,128)}, u32[]{:S(2)}) copy-start(f32[4,512]{1,0:T(4,128)} %get-tuple-element.19) | copy-start | bytes 24580
